TPU v7x, 32 devices: a whole 2x2x4 slice. The times are simulated.
32 devices in a mesh: ctx: 4 (over y, x), exp: 8 (over z, core).
Axes of the slice: x: 2, y: 2, z: 4, core: 2. Of those that a mesh axis runs over, the one named last changes fastest.
Arguments:
- residual: bfloat16 [4096, 2048], P(('ctx', 'exp')), may hold values from -6 to 6
- queries: bfloat16 [4096, 4096], P('ctx', 'exp'), may hold values from -6.5 to 6.5
- key_rows: bfloat16 [4096, 512], P('ctx'), may hold values from -6.5 to 6.5
- value_rows: bfloat16 [4096, 512], P('ctx'), may hold values from -6 to 6
- segment_ids: int32 [4096], P('ctx'), may hold values from 0 to 15, never falling along the last dimension, each value on 1 to 2304 neighbouring positions
- out_weight: bfloat16 [4096, 2048], P('exp'), may hold values from -0.09375 to 0.09375
- norm_gain: float32 [2048], replicated, may hold values from 0.5 to 1.5
- expert_ids: int32 [4096, 8], P(('ctx', 'exp')), may hold values from 0 to 31, all different within a row; in each aligned block of 128 rows (0 to 127, 128 to 255, ...) at most 64 rows name the same one
- route_weight: float32 [4096, 8], P(('ctx', 'exp')), may hold values from 0.02 to 0.3
- gate_weight: bfloat16 [32, 2048, 768], P(('ctx', 'exp')), may hold values from -0.125 to 0.125
- up_weight: bfloat16 [32, 2048, 768], P(('ctx', 'exp')), may hold values from -0.125 to 0.125
- down_weight: bfloat16 [32, 768, 2048], P(('ctx', 'exp')), may hold values from -0.21875 to 0.21875
Outputs:
- layer_out: bfloat16 [4096, 2048], P(('ctx', 'exp'))
Inputs may be any that keep to these rules, and one draw needn't show every extreme that they name: `expert_ids`: within the rows of one device (128 aligned positions), no expert is named by more than 64 rows; some expert is named by exactly 64. `segment_ids`: never falling along positions; each segment covers at most 2304 positions, and some segment exactly 2304.
All inputs are finite; a program needn't handle non-finite values.
Results may differ from a plain program's by a relative error of at most 0.013.
Values may be sent and summed in bfloat16 or wider, within the bound.
A program may use at most 128 MiB of HBM per device.

v0:
```python
import math

import jax
import jax.numpy as jnp
from jax import lax
from jax.sharding import PartitionSpec as P

HEADS = 32
KV_HEADS = 4
HEAD_DIM = 128
TOP = 8


def attend_keys(
    running, query_block, query_segs, query_anchor, key_piece, value_piece, key_segs, query_tile
):
    local_heads = query_block.shape[1] // HEAD_DIM
    query_count = query_block.shape[0] // query_tile
    key_count = key_piece.shape[0] // query_tile
    score_scale = 1.0 / math.sqrt(HEAD_DIM)
    tile_range = jnp.arange(query_tile, dtype=jnp.int32)

    def tile_step(tile_index, tile_state):
        query_begin = tile_index // key_count * query_tile
        key_begin = tile_index % key_count * query_tile
        query_part = lax.dynamic_slice_in_dim(query_block, query_begin, query_tile, 0).reshape(
            query_tile, local_heads, HEAD_DIM
        )
        part_segs = lax.dynamic_slice_in_dim(query_segs, query_begin, query_tile, 0)
        key_part = lax.dynamic_slice_in_dim(key_piece, key_begin, query_tile, 0)
        value_part = lax.dynamic_slice_in_dim(value_piece, key_begin, query_tile, 0)
        near_segs = lax.dynamic_slice_in_dim(key_segs, key_begin, query_tile, 0)
        query_pos = query_anchor + query_begin + tile_range
        key_pos = key_begin + tile_range
        reachable = (
            (key_pos[0] <= query_pos[-1])
            & (near_segs[-1] >= part_segs[0])
            & (near_segs[0] <= part_segs[-1])
        )

        def update(current):
            row_max, totals, accumulated = current
            old_max = lax.dynamic_slice_in_dim(row_max, query_begin, query_tile, 1)
            old_total = lax.dynamic_slice_in_dim(totals, query_begin, query_tile, 1)
            old_accum = lax.dynamic_slice_in_dim(accumulated, query_begin, query_tile, 0)
            scores = (
                jnp.einsum("qhd,kd->hqk", query_part, key_part, preferred_element_type=jnp.float32)
                * score_scale
            )
            visible = (part_segs[:, None] == near_segs[None, :]) & (
                key_pos[None, :] <= query_pos[:, None]
            )
            scores = jnp.where(visible[None], scores, -jnp.inf)
            new_max = jnp.maximum(old_max, jnp.max(scores, axis=-1))
            rescale = jnp.exp(old_max - new_max)
            unnormed = jnp.exp(scores - new_max[..., None])
            new_total = rescale * old_total + jnp.sum(unnormed, axis=-1)
            weights = unnormed.astype(jnp.bfloat16)
            gained = jnp.einsum(
                "hqk,kd->qhd", weights, value_part, preferred_element_type=jnp.float32
            )
            new_accum = old_accum * jnp.transpose(rescale)[:, :, None] + gained
            row_max = lax.dynamic_update_slice_in_dim(row_max, new_max, query_begin, 1)
            totals = lax.dynamic_update_slice_in_dim(totals, new_total, query_begin, 1)
            accumulated = lax.dynamic_update_slice_in_dim(accumulated, new_accum, query_begin, 0)
            return (row_max, totals, accumulated)

        def keep_state(current):
            return current

        return lax.cond(reachable, update, keep_state, tile_state)

    return lax.fori_loop(0, query_count * key_count, tile_step, running)


def expert_rows(arrived, gate_weight, up_weight, down_weight):
    in_shape = arrived.shape
    flat_rows = arrived.reshape(-1, in_shape[-1])
    gate_proj = jnp.dot(flat_rows, gate_weight[0], preferred_element_type=jnp.float32)
    up_proj = jnp.dot(flat_rows, up_weight[0], preferred_element_type=jnp.float32)
    hidden = (jax.nn.silu(gate_proj) * up_proj).astype(jnp.bfloat16)
    produced = jnp.dot(hidden, down_weight[0], preferred_element_type=jnp.float32).astype(
        jnp.bfloat16
    )
    return produced.reshape(in_shape)


def shards(
    residual,
    queries,
    key_rows,
    value_rows,
    segment_ids,
    out_weight,
    norm_gain,
    expert_ids,
    route_weight,
    gate_weight,
    up_weight,
    down_weight,
):
    ctx_rows = queries.shape[0]
    local_cols = queries.shape[1]
    local_heads = local_cols // HEAD_DIM
    group_size = HEADS // KV_HEADS
    exp_index = lax.axis_index("exp")
    ctx_index = lax.axis_index("ctx")
    ctx_count = lax.axis_size("ctx")
    exp_count = lax.axis_size("exp")
    kv_index = exp_index * local_heads // group_size
    my_keys = lax.dynamic_slice_in_dim(key_rows, kv_index * HEAD_DIM, HEAD_DIM, 1)
    my_values = lax.dynamic_slice_in_dim(value_rows, kv_index * HEAD_DIM, HEAD_DIM, 1)
    query_tile = min(512, ctx_rows)
    initial = (
        jnp.full((local_heads, ctx_rows), -1e30, jnp.float32),
        jnp.zeros((local_heads, ctx_rows), jnp.float32),
        jnp.zeros((ctx_rows, local_heads, HEAD_DIM), jnp.float32),
    )
    row_max, totals, accumulated = attend_keys(
        initial,
        queries,
        segment_ids,
        ctx_index * ctx_rows,
        lax.all_gather(my_keys, "ctx", axis=0, tiled=True),
        lax.all_gather(my_values, "ctx", axis=0, tiled=True),
        lax.all_gather(segment_ids, "ctx", axis=0, tiled=True),
        query_tile,
    )
    attended = (
        (accumulated / jnp.transpose(totals)[:, :, None])
        .reshape(ctx_rows, local_cols)
        .astype(jnp.bfloat16)
    )
    own_rows = residual.shape[0]
    attention_sum = lax.psum_scatter(
        jnp.dot(attended, out_weight, preferred_element_type=jnp.float32).astype(jnp.bfloat16),
        "exp",
        scatter_dimension=0,
        tiled=True,
    ).astype(jnp.float32)
    mixed_rows = residual.astype(jnp.float32) + attention_sum
    mean_square = jnp.mean(mixed_rows * mixed_rows, axis=-1, keepdims=True)
    normed = (mixed_rows * lax.rsqrt(mean_square + 1e-06) * norm_gain).astype(jnp.bfloat16)
    model_width = normed.shape[1]
    expert_count = ctx_count * exp_count
    capacity = 2 * own_rows * TOP // expert_count
    flat_ids = expert_ids.reshape(-1)
    onehot = (flat_ids[:, None] == jnp.arange(expert_count, dtype=jnp.int32)[None, :]).astype(
        jnp.int32
    )
    slot_index = jnp.sum(jnp.cumsum(onehot, axis=0) * onehot, axis=1) - 1
    repeated = jnp.repeat(normed, TOP, axis=0)
    outgoing = (
        jnp.zeros((expert_count, capacity, model_width), jnp.bfloat16)
        .at[flat_ids, slot_index]
        .set(repeated)
    )
    returned = lax.all_to_all(
        expert_rows(
            lax.all_to_all(outgoing, ("ctx", "exp"), split_axis=0, concat_axis=0, tiled=True),
            gate_weight,
            up_weight,
            down_weight,
        ),
        ("ctx", "exp"),
        split_axis=0,
        concat_axis=0,
        tiled=True,
    )
    fetched = returned[flat_ids, slot_index].astype(jnp.float32) * route_weight.reshape(-1)[:, None]
    routed = jnp.sum(fetched.reshape(own_rows, TOP, model_width), axis=1)
    return (mixed_rows + routed).astype(jnp.bfloat16)


def solution(mesh):
    return jax.shard_map(
        shards,
        mesh=mesh,
        in_specs=(
            P(("ctx", "exp"), None),
            P("ctx", "exp"),
            P("ctx", None),
            P("ctx", None),
            P("ctx"),
            P("exp", None),
            P(),
            P(("ctx", "exp"), None),
            P(("ctx", "exp"), None),
            P(("ctx", "exp"), None, None),
            P(("ctx", "exp"), None, None),
            P(("ctx", "exp"), None, None),
        ),
        out_specs=P(("ctx", "exp"), None),
        check_vma=False,
    )
```

profile of v0, /device:TPU:0, one launch (start us, length us, event | category | flops | bytes accessed | tf_op | source)
XLA Modules:
  0.0 883.7 jit_solution(13812402135413184145)
XLA Ops:
  6.5 1.8 constant_dynamic-slice_fusion.2
  8.4 1.7 constant_dynamic-slice_fusion.1
  10.2 2.3 copy.27
  12.5 9.7 %all_gather.9 = s32[4096]{0:T(1024)S(1)} all-gather(s32[1024]{0:T(1024)} %param.20), channel_id=1, replica_groups=mesh['ctx'=4,'exp'=8] {'ctx'}, dimensions={0}, use_global_device_ids=true | all-gather | bytes 20480 | tf_op jit(solution)/shard_map/all_gather | solution.py:126
  22.2 16.3 %all-gather.3.cloned.1.call-done = bf16[4096,128]{1,0:T(8,128)(2,1)} async-done(((bf16[1024,128]{1,0:T(8,128)(2,1)}), bf16[4096,128]{1,0:T(8,128)(2,1)}) %all-gather.3.cloned.1.call-update) | async-done | bytes 1048592 | tf_op jit(solution)/shard_map/all_gather | solution.py:124
  38.6 28.5 %all-gather.5.cloned.1.call-done = bf16[4096,128]{1,0:T(8,128)(2,1)} async-done(((bf16[1024,128]{1,0:T(8,128)(2,1)}), bf16[4096,128]{1,0:T(8,128)(2,1)}) %all-gather.5.cloned.1.call-update) | async-done | bytes 1048592 | tf_op jit(solution)/shard_map/all_gather | solution.py:125
  67.1 1.4 broadcast_in_dim.49
  68.5 142.6 %while.21 = (s32[]{:T(128)}, f32[4,1024]{1,0:T(4,128)S(1)}, f32[4,1024]{1,0:T(4,128)S(1)}, f32[1024,4,128]{2,0,1:T(8,128)}, s32[]{:T(128)}, /*index=5*/s32[4096]...) while((s32[]{:T(128)}, f32[4,1024]{1,0:T(4,128)S(1)}, ...), condition=%wide.region_5.6_spmd.clone.clone, body=%wide.region_0.5_spmd.clone.clone.sunk | while | flops 549723136 | bytes 44996356 | solution.py:73
  68.7 0.6 fusion.47
  72.2 0.6 slice.95
  74.0 18.8 %conditional.4 = ((f32[4,1024]{1,0:T(4,128)S(1)}, f32[4,1024]{1,0:T(4,128)S(1)}, f32[1024,4,128]{2,0,1:T(8,128)})) conditional(s32[]{:T(128)} %bitcast.73, (f32[4,1024]{1,0:T(4,128)S(1)}, f32[4,1024]{1,0:T(4,128)S(1)}, f32[1024,4,128]{2,0,1:T(8,128)}) %tuple.77, (s32[]{:T(128)}, f32[4,1024]{1,0:T(4,128)S(1)}, s32[512]{0:T(512)S(1)}, ...), branch_computations={%region_1.1_spmd, %region_2.4_spmd} | conditional | flops 549722112 | bytes 44983448 | solution.py:71
  74.3 1.5 constant_dynamic-slice_fusion
  75.9 1.8 fusion.4
  77.7 1.8 copy-done.2
  79.6 3.3 fusion.11
  82.9 6.1 dynamic_update_slice.14
  89.0 3.1 fusion.3
  96.4 0.6 slice.95
  101.9 0.6 slice.95
  107.4 0.6 slice.95
  112.9 0.6 slice.95
  118.4 0.6 slice.95
  123.9 0.6 slice.95
  129.4 0.6 slice.95
  134.9 0.6 slice.95
  136.8 17.9 %conditional.4 = ((f32[4,1024]{1,0:T(4,128)S(1)}, f32[4,1024]{1,0:T(4,128)S(1)}, f32[1024,4,128]{2,0,1:T(8,128)})) conditional(s32[]{:T(128)} %bitcast.73, (f32[4,1024]{1,0:T(4,128)S(1)}, f32[4,1024]{1,0:T(4,128)S(1)}, f32[1024,4,128]{2,0,1:T(8,128)}) %tuple.77, (s32[]{:T(128)}, f32[4,1024]{1,0:T(4,128)S(1)}, s32[512]{0:T(512)S(1)}, ...), branch_computations={%region_1.1_spmd, %region_2.4_spmd} | conditional | flops 549722112 | bytes 44983448 | solution.py:71
  137.1 1.5 constant_dynamic-slice_fusion
  138.6 1.8 fusion.4
  140.4 1.8 copy-done.2
  142.3 3.3 fusion.11
  145.5 5.5 dynamic_update_slice.14
  151.0 3.1 fusion.3
  158.4 0.6 slice.95
  160.2 17.9 %conditional.4 = ((f32[4,1024]{1,0:T(4,128)S(1)}, f32[4,1024]{1,0:T(4,128)S(1)}, f32[1024,4,128]{2,0,1:T(8,128)})) conditional(s32[]{:T(128)} %bitcast.73, (f32[4,1024]{1,0:T(4,128)S(1)}, f32[4,1024]{1,0:T(4,128)S(1)}, f32[1024,4,128]{2,0,1:T(8,128)}) %tuple.77, (s32[]{:T(128)}, f32[4,1024]{1,0:T(4,128)S(1)}, s32[512]{0:T(512)S(1)}, ...), branch_computations={%region_1.1_spmd, %region_2.4_spmd} | conditional | flops 549722112 | bytes 44983448 | solution.py:71
  160.5 1.5 constant_dynamic-slice_fusion
  162.0 1.8 fusion.4
  163.9 1.8 copy-done.2
  165.7 3.3 fusion.11
  169.0 5.5 dynamic_update_slice.14
  174.5 3.1 fusion.3
  181.8 0.6 slice.95
  187.3 0.6 slice.95
  192.8 0.6 slice.95
  198.3 0.6 slice.95
  203.8 0.6 slice.95
  209.3 0.6 slice.95
  211.2 2.9 copy.28
  214.1 1.9 divide_convert_fusion
  215.9 5.9 convolution_convert_fusion.1
  221.9 0.7 copy-done.9
  222.9 9.0 %reduce-window.6 = s32[32,8,128]{2,1,0:T(8,128)S(1)} reduce-window(s32[32,8,128]{2,1,0:T(8,128)S(1)} %fusion.37, s32[]{:T(128)} %constant.171.clone.1), window={size=1x1x128 pad=0_0x0_0x127_0}, to_apply=%region_7.8 | reduce-window | flops 4161536 | bytes 262148 | tf_op jit(solution)/shard_map/reduce-window
  232.7 186.0 %reduce-scatter.2.cloned.1.call-done = bf16[128,2048]{1,0:T(8,128)(2,1)} async-done(((bf16[1024,2048]{1,0:T(8,128)(2,1)}), bf16[128,2048]{1,0:T(8,128)(2,1)}) %reduce-scatter.2.cloned.1.call-update) | async-done | bytes 524304 | tf_op jit(solution)/shard_map/reduce_scatter | solution.py:135
  418.8 1.5 multiply_reduce_fusion
  420.2 2.2 multiply_convert_fusion.1
  422.4 11.9 %scatter_custom_fusion = bf16[2048,2048]{1,0:T(8,128)(2,1)} fusion(s32[1024]{0:T(1024)S(1)} %broadcast_select_fusion, bf16[]{:T(256)} %constant.184.clone.1, bf16[128,2048]{1,0:T(8,128)(2,1)} %multiply_convert_fusion.1), kind=kCustom, calls=%fused_computation.33 | custom fusion | bytes 8912898
  434.3 188.0 %all_to_all.10 = bf16[32,64,2048]{2,1,0:T(8,128)(2,1)S(1)} all-to-all(bf16[32,64,2048]{2,1,0:T(8,128)(2,1)} %bitcast.76), channel_id=1, replica_groups=mesh['ctx'=4,'exp'=8] {'ctx','exp'}, dimensions={0} | all-to-all | bytes 16777216 | tf_op jit(solution)/shard_map/all_to_all | solution.py:160
  622.3 3.2 copy-done.3
  625.6 8.5 fusion.31
  634.1 21.3 %convolution_convert_fusion = bf16[2048,2048]{1,0:T(8,128)(2,1)} fusion(f32[2048,768]{1,0:T(8,128)} %fusion.31, bf16[2048,2048]{1,0:T(8,128)(2,1)} %bitcast.79, bf16[1,768,2048]{2,1,0:T(8,128)(2,1)S(1)} %copy-done, bf16[1,2048,768]{2,1,0:T(8,128)(2,1)} %param.26), kind=kOutput, calls=%fused_computation.31 | convolution fusion | flops 12898533376 | bytes 29360128 | tf_op jit(solution)/shard_map/dot_general | solution.py:82
  655.3 4.1 all-to-all-start.1
  659.5 184.5 %all-to-all-done.1 = bf16[32,64,2048]{2,1,0:T(8,128)(2,1)} async-done(((bf16[32,64,2048]{2,1,0:T(8,128)(2,1)}), bf16[32,64,2048]{2,1,0:T(8,128)(2,1)}, u32[]{:S(2)}, u32[]{:S(2)}) %all-to-all-start.1) | async-done | bytes 8388640 | tf_op jit(solution)/shard_map/all_to_all | solution.py:158
  844.1 25.5 %gather_fusion = bf16[1024,2048]{1,0:T(8,128)(2,1)} fusion(bf16[32,64,2048]{2,1,0:T(8,128)(2,1)} %all-to-all-done.1, s32[1024]{0:T(1024)S(1)} %bitcast.74), kind=kCustom, calls=%fused_computation | custom fusion | bytes 8396800 | tf_op jit(solution)/shard_map/gather | solution.py:170
  869.6 6.6 fusion.24
  876.2 1.0 add_convert_fusion
  (165 shorter events, 23.9 us)
Async XLA Ops:
  6.5 627.5 %copy-start = (bf16[1,768,2048]{2,1,0:T(8,128)(2,1)S(1)}, bf16[1,768,2048]{2,1,0:T(8,128)(2,1)}, u32[]{:S(2)}) copy-start(bf16[1,768,2048]{2,1,0:T(8,128)(2,1)} %param.27) | copy-start | bytes 9437188
  6.5 62.0 %copy-start.7 = (s32[1024]{0:T(1024)S(1)}, s32[1024]{0:T(1024)}, u32[]{:S(2)}) copy-start(s32[1024]{0:T(1024)} %param.20) | copy-start | bytes 12292
  6.5 32.0 %all-gather.3.cloned.1.call-start = ((), (), s32[]{:S(2)}) async-start(), calls=%async_computation.3 | async-start | bytes 1310720 | tf_op jit(solution)/shard_map/all_gather | solution.py:124
  8.4 58.7 %all-gather.5.cloned.1.call-start = ((), (), s32[]{:S(2)}) async-start(), calls=%async_computation.4 | async-start | bytes 1310720 | tf_op jit(solution)/shard_map/all_gather | solution.py:125
  10.1 408.6 %reduce-scatter.2.cloned.1.call-start = ((), (), s32[]{:S(2)}) async-start(), calls=%async_computation.5 | async-start | bytes 4718592 | tf_op jit(solution)/shard_map/reduce_scatter | solution.py:135
  74.0 5.5 copy-start.4
  77.6 1.9 copy-start.2
  136.8 5.5 copy-start.4
  140.3 1.9 copy-start.2
  160.2 5.5 copy-start.4
  163.8 1.9 copy-start.2
  221.9 0.7 copy-start.9
  221.9 10.6 %copy-start.12 = (s32[2]{0:T(128)S(1)}, s32[2]{0:T(128)}, u32[]{:S(2)}) copy-start(s32[2]{0:T(128)} %constant.193) | copy-start | bytes 28
  221.9 10.7 %copy-start.11 = (s32[2]{0:T(128)S(1)}, s32[2]{0:T(128)}, u32[]{:S(2)}) copy-start(s32[2]{0:T(128)} %constant.196) | copy-start | bytes 28
  221.9 198.4 %copy-start.8 = (f32[2048]{0:T(1024)S(1)}, f32[2048]{0:T(1024)}, u32[]{:S(2)}) copy-start(f32[2048]{0:T(1024)} %param.22) | copy-start | bytes 24580
  434.3 191.3 %copy-start.13 = (bf16[1,2048,768]{2,1,0:T(8,128)(2,1)S(1)}, bf16[1,2048,768]{2,1,0:T(8,128)(2,1)}, u32[]{:S(2)}) copy-start(bf16[1,2048,768]{2,1,0:T(8,128)(2,1)} %param.25) | copy-start | bytes 9437188
  622.3 3.2 copy-start.3
  655.3 4.1 copy-start.10
  655.3 188.7 %all-to-all-start.1 = ((bf16[32,64,2048]{2,1,0:T(8,128)(2,1)}), bf16[32,64,2048]{2,1,0:T(8,128)(2,1)}, u32[]{:S(2)}, u32[]{:S(2)}) async-start(bf16[32,64,2048]{2,1,0:T(8,128)(2,1)} %bitcast.77), calls=%async_computation.2 | async-start | bytes 16777216 | tf_op jit(solution)/shard_map/all_to_all | solution.py:158
  844.1 33.1 %copy-start.1 = (bf16[1,768,2048]{2,1,0:T(8,128)(2,1)S(1)}, bf16[1,768,2048]{2,1,0:T(8,128)(2,1)}, u32[]{:S(2)}) copy-start(bf16[1,768,2048]{2,1,0:T(8,128)(2,1)} %param.27) | copy-start | bytes 9437188
  869.6 6.6 copy-start.5
  869.6 6.6 copy-start.6
Sparse Core Ops, SparseCore 0:
  9.2 29.3 all-gather.2
  40.4 26.6 all-gather.4
  222.0 196.6 reduce-scatter.1
where the time goes:
time: 869 us; the launch traced here: 884 us
  waiting for transfers between devices  415 us (48%)
  blocking collectives  198 us (23%)
  local copies, waits for them, and re-layouts  111 us (13%)
  loops' own time  57.9 us (7%)
  matrix products  50.8 us (6%)
  other arithmetic  33.2 us (4%)
  between operations  13.3 us (2%)
    all_to_all x1, blocking collectives, shards(): lax.all_to_all(outgoing, ('ctx', 'exp'), split_axis=0, concat_axis=0, til...  188 us
    reduce_scatter x1, waiting for transfers between devices, shards(): lax.psum_scatter(jnp.dot(attended, out_weight, preferred_element_type=jnp...  186 us
    all_to_all x1, waiting for transfers between devices, shards(): lax.all_to_all(expert_rows(lax.all_to_all(outgoing, ('ctx', 'exp'), split...  185 us
    another operation x1, loops' own time, attend_keys(): return lax.fori_loop(0, query_count * key_count, tile_step, running)  57.5 us
    all_gather x1, waiting for transfers between devices, shards(): lax.all_gather(my_values, 'ctx', axis=0, tiled=True)  28.5 us
    gather x1, local copies, waits for them, and re-layouts, shards(): returned[flat_ids, slot_index].astype(jnp.float32)  25.5 us
    dot_general x1, matrix products, expert_rows(): jnp.dot(hidden, down_weight[0], preferred_element_type=jnp.float32)  21.3 us
    unnamed x28, local copies, waits for them, and re-layouts  18.3 us
  transfers between devices with their start and end apart: 4, of which 4 were waited for; matrix products, arithmetic and copies ran while one was open for 2% of the time, Pallas kernels for 0%

commit v1 on v0

v1 whole, which is shorter than its diff:
```python
import functools
import math

import jax
import jax.numpy as jnp
from jax import lax
from jax.experimental import pallas as pl
from jax.experimental.pallas import tpu as pltpu
from jax.sharding import PartitionSpec as P

HEADS = 32
KV_HEADS = 4
HEAD_DIM = 128
TOP = 8
QUERY_TILE = 256
KEY_TILE = 256
LOW = -1e30
DENSE_BYTES = 32 * 1024 * 1024


def attention_kernel(
    tile_rows, heads, bounds_ref, q_ref, start_ref, k_ref, v_ref, w_ref, out_ref, m_ref, l_ref, acc_ref
):
    tile = pl.program_id(0)
    first = bounds_ref[0, tile]
    last = bounds_ref[1, tile]
    query_begin = bounds_ref[2, tile]
    scale = math.log2(math.e) / math.sqrt(HEAD_DIM)
    m_ref[...] = jnp.full_like(m_ref, LOW)
    l_ref[...] = jnp.zeros_like(l_ref)
    acc_ref[...] = jnp.zeros_like(acc_ref)
    starts = start_ref[...]
    query_pos = query_begin + lax.broadcasted_iota(jnp.int32, (1, tile_rows), 1)

    @pl.loop(first, last)
    def _(key_tile):
        key_begin = pl.multiple_of(key_tile * KEY_TILE, KEY_TILE)
        keys = k_ref[pl.ds(key_begin, KEY_TILE), :]
        values = v_ref[pl.ds(key_begin, KEY_TILE), :]
        key_pos = key_begin + lax.broadcasted_iota(jnp.int32, (KEY_TILE, 1), 0)
        visible = (key_pos >= starts) & (key_pos <= query_pos)
        for head in range(heads):
            query = q_ref[:, head * HEAD_DIM : (head + 1) * HEAD_DIM]
            scores = lax.dot_general(
                keys, query, (((1,), (1,)), ((), ())), preferred_element_type=jnp.float32
            )
            scores = jnp.where(visible, scores * scale, LOW * 2)
            old_max = m_ref[head : head + 1, :]
            new_max = jnp.maximum(old_max, jnp.max(scores, axis=0, keepdims=True))
            rescale = jnp.exp2(old_max - new_max)
            unnormed = jnp.exp2(scores - new_max)
            l_ref[head : head + 1, :] = l_ref[head : head + 1, :] * rescale + jnp.sum(
                unnormed, axis=0, keepdims=True
            )
            m_ref[head : head + 1, :] = new_max
            gained = lax.dot_general(
                values,
                unnormed.astype(jnp.bfloat16),
                (((0,), (0,)), ((), ())),
                preferred_element_type=jnp.float32,
            )
            rows = slice(head * HEAD_DIM, (head + 1) * HEAD_DIM)
            acc_ref[rows, :] = acc_ref[rows, :] * rescale + gained

    for head in range(heads):
        rows = slice(head * HEAD_DIM, (head + 1) * HEAD_DIM)
        acc_ref[rows, :] = acc_ref[rows, :] / l_ref[head : head + 1, :]
    attended = acc_ref[...].T.astype(jnp.bfloat16)
    out_ref[...] = jnp.dot(attended, w_ref[...], preferred_element_type=jnp.float32).astype(
        jnp.bfloat16
    )


def attend(queries, starts, bounds, keys, values, out_weight):
    rows, columns = queries.shape
    heads = columns // HEAD_DIM
    width = out_weight.shape[1]
    tile = min(QUERY_TILE, rows)
    whole = lambda i, bounds: (0, 0)
    return pl.pallas_call(
        functools.partial(attention_kernel, tile, heads),
        out_shape=jax.ShapeDtypeStruct((rows, width), jnp.bfloat16),
        grid_spec=pltpu.PrefetchScalarGridSpec(
            num_scalar_prefetch=1,
            grid=(rows // tile,),
            in_specs=[
                pl.BlockSpec((tile, columns), lambda i, bounds: (i, 0)),
                pl.BlockSpec((1, tile), lambda i, bounds: (0, i)),
                pl.BlockSpec(keys.shape, whole),
                pl.BlockSpec(values.shape, whole),
                pl.BlockSpec(out_weight.shape, whole),
            ],
            out_specs=pl.BlockSpec((tile, width), lambda i, bounds: (i, 0)),
            scratch_shapes=[
                pltpu.VMEM((heads, tile), jnp.float32),
                pltpu.VMEM((heads, tile), jnp.float32),
                pltpu.VMEM((columns, tile), jnp.float32),
            ],
        ),
        compiler_params=pltpu.CompilerParams(vmem_limit_bytes=48 * 1024 * 1024),
    )(bounds, queries, starts, keys, values, out_weight)


def gather_rows(rows):
    return lax.all_gather(rows, ("ctx", "exp"), axis=0, tiled=True)


def scatter_sum(partial):
    return lax.psum_scatter(partial, ("ctx", "exp"), scatter_dimension=0, tiled=True)


def route_slots(expert_ids, route_weight, expert_count):
    own_rows = expert_ids.shape[0]
    experts = jnp.arange(expert_count, dtype=jnp.int32)
    route_table = jnp.sum(
        jnp.where(experts[:, None, None] == expert_ids[None], route_weight[None], 0.0), axis=-1
    )
    my_route = lax.all_to_all(
        route_table, ("ctx", "exp"), split_axis=0, concat_axis=0, tiled=True
    )
    capacity = 2 * own_rows * TOP // expert_count
    hits = my_route > 0
    slot = jnp.cumsum(hits.astype(jnp.int32), axis=1) - 1
    picked = hits[:, None, :] & (
        slot[:, None, :] == jnp.arange(capacity, dtype=jnp.int32)[None, :, None]
    )
    pick = picked.astype(jnp.bfloat16)
    slot_weight = jnp.sum(jnp.where(picked, my_route[:, None, :], 0.0), axis=-1)
    return pick, slot_weight


def apply_expert(arrived, gate_weight, up_weight, down_weight):
    gate_proj = jnp.dot(arrived, gate_weight[0], preferred_element_type=jnp.float32)
    up_proj = jnp.dot(arrived, up_weight[0], preferred_element_type=jnp.float32)
    hidden = (jax.nn.silu(gate_proj) * up_proj).astype(jnp.bfloat16)
    return jnp.dot(hidden, down_weight[0], preferred_element_type=jnp.float32)


def dense_experts(normed, pick, slot_weight, gate_weight, up_weight, down_weight):
    expert_count, capacity, own_rows = pick.shape
    width = normed.shape[1]
    everyone = gather_rows(normed).reshape(expert_count, own_rows, width)
    arrived = jnp.einsum(
        "bsr,brd->bsd", pick, everyone, preferred_element_type=jnp.bfloat16
    ).reshape(-1, width)
    produced = apply_expert(arrived, gate_weight, up_weight, down_weight)
    weighted = (produced * slot_weight.reshape(-1, 1)).astype(jnp.bfloat16)
    partial = jnp.einsum(
        "bsr,bsd->brd",
        pick,
        weighted.reshape(expert_count, capacity, width),
        preferred_element_type=jnp.bfloat16,
    ).reshape(-1, width)
    return scatter_sum(partial).astype(jnp.float32)


def slot_experts(
    normed, expert_ids, route_weight, gate_weight, up_weight, down_weight, expert_count
):
    own_rows, width = normed.shape
    capacity = 2 * own_rows * TOP // expert_count
    flat_ids = expert_ids.reshape(-1)
    experts = jnp.arange(expert_count, dtype=jnp.int32)
    onehot = (flat_ids[:, None] == experts[None, :]).astype(jnp.int32)
    slot_index = jnp.sum(jnp.cumsum(onehot, axis=0) * onehot, axis=1) - 1
    outgoing = (
        jnp.zeros((expert_count, capacity, width), jnp.bfloat16)
        .at[flat_ids, slot_index]
        .set(jnp.repeat(normed, TOP, axis=0))
    )
    swap = functools.partial(
        lax.all_to_all, axis_name=("ctx", "exp"), split_axis=0, concat_axis=0, tiled=True
    )
    arrived = swap(outgoing)
    produced = apply_expert(arrived.reshape(-1, width), gate_weight, up_weight, down_weight)
    returned = swap(produced.astype(jnp.bfloat16).reshape(arrived.shape))
    fetched = returned[flat_ids, slot_index].astype(jnp.float32)
    fetched = fetched * route_weight.reshape(-1)[:, None]
    return jnp.sum(fetched.reshape(own_rows, TOP, width), axis=1)


def shards(
    residual,
    queries,
    key_rows,
    value_rows,
    segment_ids,
    out_weight,
    norm_gain,
    expert_ids,
    route_weight,
    gate_weight,
    up_weight,
    down_weight,
):
    ctx_rows = queries.shape[0]
    local_heads = queries.shape[1] // HEAD_DIM
    group_size = HEADS // KV_HEADS
    exp_index = lax.axis_index("exp")
    ctx_index = lax.axis_index("ctx")
    expert_count = lax.axis_size("ctx") * lax.axis_size("exp")
    kv_index = exp_index * local_heads // group_size
    my_keys = lax.dynamic_slice_in_dim(key_rows, kv_index * HEAD_DIM, HEAD_DIM, 1)
    my_values = lax.dynamic_slice_in_dim(value_rows, kv_index * HEAD_DIM, HEAD_DIM, 1)
    both = lax.all_gather(
        jnp.concatenate([my_keys, my_values], axis=1), "ctx", axis=0, tiled=True
    )
    all_segs = lax.all_gather(segment_ids, "ctx", axis=0, tiled=True)

    own_rows = residual.shape[0]
    if expert_count * own_rows * residual.shape[1] * 2 <= DENSE_BYTES:
        pick, slot_weight = route_slots(expert_ids, route_weight, expert_count)

    starts = jnp.sum((all_segs[:, None] < segment_ids[None, :]).astype(jnp.int32), axis=0)
    tile = min(QUERY_TILE, ctx_rows)
    begins = ctx_index * ctx_rows + jnp.arange(ctx_rows // tile, dtype=jnp.int32) * tile
    bounds = jnp.stack([starts[::tile] // KEY_TILE, (begins + tile - 1) // KEY_TILE + 1, begins])
    head_terms = attend(
        queries,
        starts.reshape(1, -1),
        bounds.astype(jnp.int32),
        both[:, :HEAD_DIM],
        both[:, HEAD_DIM:],
        out_weight,
    )
    attention_sum = lax.psum_scatter(
        head_terms, "exp", scatter_dimension=0, tiled=True
    ).astype(jnp.float32)
    mixed_rows = residual.astype(jnp.float32) + attention_sum
    mean_square = jnp.mean(mixed_rows * mixed_rows, axis=-1, keepdims=True)
    normed = (mixed_rows * lax.rsqrt(mean_square + 1e-06) * norm_gain).astype(jnp.bfloat16)
    width = normed.shape[1]

    if expert_count * own_rows * width * 2 <= DENSE_BYTES:
        routed = dense_experts(normed, pick, slot_weight, gate_weight, up_weight, down_weight)
    else:
        routed = slot_experts(
            normed, expert_ids, route_weight, gate_weight, up_weight, down_weight, expert_count
        )
    return (mixed_rows + routed).astype(jnp.bfloat16)


def solution(mesh):
    return jax.shard_map(
        shards,
        mesh=mesh,
        in_specs=(
            P(("ctx", "exp"), None),
            P("ctx", "exp"),
            P("ctx", None),
            P("ctx", None),
            P("ctx"),
            P("exp", None),
            P(),
            P(("ctx", "exp"), None),
            P(("ctx", "exp"), None),
            P(("ctx", "exp"), None, None),
            P(("ctx", "exp"), None, None),
            P(("ctx", "exp"), None, None),
        ),
        out_specs=P(("ctx", "exp"), None),
        check_vma=False,
    )
```

time: 869 us -> 507 us (0.58); the launches traced: 884 us -> 507 us
  blocking collectives: 198 us -> 19.4 us
  local copies, waits for them, and re-layouts: 111 us -> 5.89 us
  loops' own time: 57.9 us -> 0 us
  waiting for transfers between devices: 415 us -> 384 us
  other arithmetic: 33.2 us -> 10.4 us
  Pallas kernels: 0 us -> 17.5 us
    all_to_all x1 -> x0, waiting for transfers between devices: 185 us -> none  [shards(): lax.all_to_all(expert_rows(lax.all_to_all(outgoing, ('ctx', 'exp'), split...]
    all_to_all x1, blocking collectives: 188 us -> 9.7 us  [route_slots(): lax.all_to_all(route_table, ('ctx', 'exp'), split_axis=0, concat_axis=0,...]
    all_gather x2, waiting for transfers between devices: 44.8 us -> 129 us  [the longest x1 103 us: gather_rows(): return lax.all_gather(rows, ('ctx', 'exp'), axis=0, tiled=True)]
    reduce_scatter x1 -> x2, waiting for transfers between devices: 186 us -> 255 us  [the longest x1 185 us: scatter_sum(): lax.psum_scatter(partial, ('ctx', 'exp'), scatter_dimension=0, tiled=True)]
    another operation x17 -> x0, loops' own time: 57.9 us -> none  [the longest x1 57.5 us: attend_keys(): return lax.fori_loop(0, query_count * key_count, tile_step, running)]
    slice x48 -> x2, local copies, waits for them, and re-layouts: 27.8 us -> 1.76 us  [the longest x1 1.68 us: shards(): both[:, HEAD_DIM:]]
    gather x1 -> x0, local copies, waits for them, and re-layouts: 25.5 us -> none  [shards(): returned[flat_ids, slot_index].astype(jnp.float32)]
    dynamic_update_slice x9 -> x0, local copies, waits for them, and re-layouts: 18.6 us -> none  [the longest x3 17.1 us: update(): lax.dynamic_update_slice_in_dim(accumulated, new_accum, query_begin, 0)]
  transfers between devices with their start and end apart: 4 -> 4, of which waited for: 4 -> 4; matrix products, arithmetic and copies ran while one was open for 2% -> 1% of each run, Pallas kernels for 0% -> 0%
where the time goes in v1:
time: 507 us
  waiting for transfers between devices  384 us (76%)
  matrix products  56.4 us (11%)
  blocking collectives  19.4 us (4%)
  Pallas kernels  17.5 us (3%)
  between operations  13.2 us (3%)
  other arithmetic  10.4 us (2%)
  local copies, waits for them, and re-layouts  5.89 us (1%)
    reduce_scatter x1, waiting for transfers between devices, scatter_sum(): lax.psum_scatter(partial, ('ctx', 'exp'), scatter_dimension=0, tiled=True)  185 us
    all_gather x1, waiting for transfers between devices, gather_rows(): return lax.all_gather(rows, ('ctx', 'exp'), axis=0, tiled=True)  103 us
    reduce_scatter x1, waiting for transfers between devices, shards(): lax.psum_scatter(head_terms, 'exp', scatter_dimension=0, tiled=True)  70.3 us
    all_gather x1, waiting for transfers between devices, shards(): lax.all_gather(jnp.concatenate([my_keys, my_values], axis=1), 'ctx', axis...  26.1 us
    dot_general x1, matrix products, apply_expert(): return jnp.dot(hidden, down_weight[0], preferred_element_type=jnp.float32)  20.6 us
    pallas_call x1, Pallas kernels, attend(): pl.pallas_call(functools.partial(attention_kernel, tile, heads), out_shap...  17.5 us
    dot_general x1, matrix products, dense_experts(): jnp.einsum('bsr,bsd->brd', pick, weighted.reshape(expert_count, capacity,...  13.7 us
    dot_general x1, matrix products, dense_experts(): jnp.einsum('bsr,brd->bsd', pick, everyone, preferred_element_type=jnp.bfl...  11.5 us
  transfers between devices with their start and end apart: 4, of which 4 were waited for; matrix products, arithmetic and copies ran while one was open for 1% of the time, Pallas kernels for 0%

profile of v1, /device:TPU:0, one launch (start us, length us, event | category | flops | bytes accessed | tf_op | source)
XLA Modules:
  0.0 506.9 jit_solution(8980877929831662978)
XLA Ops:
  6.5 0.0 copy-start
  6.5 0.0 all-gather.3.cloned.1.call-start
  6.5 1.2 constant_dynamic-slice_fusion
  7.8 0.9 pad_maximum_fusion
  8.6 0.0 all-gather.3.cloned.1.call-update
  8.6 0.0 reduce-scatter.3.cloned.1.call-start
  8.7 9.7 %all_gather.9 = s32[4096]{0:T(1024)S(1)} all-gather(s32[1024]{0:T(1024)} %param.16), channel_id=1, replica_groups=mesh['ctx'=4,'exp'=8] {'ctx'}, dimensions={0}, use_global_device_ids=true | all-gather | bytes 20480 | tf_op jit(solution)/shard_map/all_gather | solution.py:208
  18.4 2.6 convert_reduce_fusion
  21.1 0.1 slice.9
  21.2 26.1 %all-gather.3.cloned.1.call-done = bf16[4096,256]{1,0:T(8,128)(2,1)} async-done(((bf16[1024,256]{1,0:T(8,128)(2,1)}), bf16[4096,256]{1,0:T(8,128)(2,1)}) %all-gather.3.cloned.1.call-update) | async-done | bytes 2097168 | tf_op jit(solution)/shard_map/all_gather | solution.py:205
  47.3 1.7 fusion.19
  49.0 0.0 copy-start.2
  49.0 1.6 copy-done.2
  50.6 0.0 copy-start.3
  50.6 1.2 copy-done.3
  51.8 0.0 copy-start.4
  51.8 0.0 copy-start.5
  51.8 0.0 copy-start.6
  51.8 17.5 %shard_map.118 = bf16[1024,2048]{1,0:T(8,128)(2,1)} custom-call(s32[3,4]{1,0:T(4,128)S(1)} %pad_add_fusion.bounds_ref, bf16[1024,512]{1,0:T(8,128)(2,1)S(1)} %copy-done.3, s32[1,1024]{1,0:T(1,128)S(1)} %bitcast.29, bf16[4096,128]{1,0:T(8,128)(2,1)S(1)} %get-tuple-element.8.k_ref, bf16[4096,128]{1,0:T(8,128)(2,1)S(1)} %get-tuple-element.7.v_ref, ...), custom_call_target="tpu_custom_call" | custom-call | tf_op jit(solution)/shard_map/pallas_call | solution.py:80
  69.3 0.0 reduce-scatter.3.cloned.1.call-update
  69.3 0.0 all-gather.5.cloned.1.call-start
  69.3 70.3 %reduce-scatter.3.cloned.1.call-done = bf16[128,2048]{1,0:T(8,128)(2,1)} async-done(((bf16[1024,2048]{1,0:T(8,128)(2,1)}), bf16[128,2048]{1,0:T(8,128)(2,1)}) %reduce-scatter.3.cloned.1.call-update) | async-done | bytes 524304 | tf_op jit(solution)/shard_map/reduce_scatter | solution.py:226
  139.6 1.5 multiply_reduce_fusion
  141.1 0.0 copy-done.4
  141.1 2.2 multiply_convert_fusion.2
  143.3 0.0 all-gather.5.cloned.1.call-update
  143.3 0.0 reduce-scatter.5.cloned.1.call-start
  143.4 0.0 copy-done.5
  143.4 0.0 copy-done.6
  143.4 9.7 %all_to_all.12 = f32[32,1,128]{2,1,0:T(1,128)S(1)} all-to-all(f32[32,1,128]{2,1,0:T(1,128)S(1)} %bitcast.37), channel_id=1, replica_groups=mesh['ctx'=4,'exp'=8] {'ctx','exp'}, dimensions={0} | all-to-all | bytes 32768 | tf_op jit(solution)/shard_map/all_to_all | solution.py:118
  153.2 0.3 reduce_window_sum.14
  153.4 0.4 select_reduce_fusion
  153.9 0.1 mul.71
  154.0 102.6 %all-gather.5.cloned.1.call-done = bf16[4096,2048]{1,0:T(8,128)(2,1)} async-done(((bf16[128,2048]{1,0:T(8,128)(2,1)}), bf16[4096,2048]{1,0:T(8,128)(2,1)}) %all-gather.5.cloned.1.call-update) | async-done | bytes 16777232 | tf_op jit(solution)/shard_map/all_gather | solution.py:105
  256.5 0.0 copy-start.7
  256.5 11.5 %fusion.9 = bf16[32,64,2048]{2,1,0:T(8,128)(2,1)} fusion(bf16[32,128,2048]{2,1,0:T(8,128)(2,1)} %bitcast.31, s32[32,128]{1,0:T(8,128)S(1)} %broadcast_add_fusion, pred[32,128]{1,0:T(8,128)(4,1)S(1)} %get-tuple-element.6), kind=kOutput, calls=%fused_computation.16 | convolution fusion | flops 1074266112 | bytes 25186304 | tf_op jit(solution)/shard_map/bsr,brd->bsd/dot_general | solution.py:143
  268.0 0.0 copy-done.7
  268.0 10.7 %fusion.3 = f32[2048,768]{1,0:T(8,128)} fusion(bf16[2048,2048]{1,0:T(8,128)(2,1)} %bitcast.33, bf16[1,2048,768]{2,1,0:T(8,128)(2,1)S(1)} %copy-done.7), kind=kOutput, calls=%fused_computation.5 | convolution fusion | flops 6442450944 | bytes 17825792 | tf_op jit(solution)/shard_map/dot_general | solution.py:133
  278.7 0.0 copy-done
  278.7 20.6 %multiply_convert_fusion = bf16[2048,2048]{1,0:T(8,128)(2,1)} fusion(f32[2048]{0:T(1024)S(1)} %mul.71, f32[2048,768]{1,0:T(8,128)} %fusion.3, bf16[2048,2048]{1,0:T(8,128)(2,1)} %bitcast.34, bf16[1,768,2048]{2,1,0:T(8,128)(2,1)S(1)} %copy-done, bf16[1,2048,768]{2,1,0:T(8,128)(2,1)} %param.22), kind=kOutput, calls=%fused_computation | convolution fusion | flops 12902727680 | bytes 29368320 | tf_op jit(solution)/shard_map/dot_general | solution.py:136
  299.3 13.7 %fusion.7 = bf16[32,128,2048]{2,1,0:T(8,128)(2,1)} fusion(bf16[32,64,2048]{2,1,0:T(8,128)(2,1)} %bitcast.32, s32[32,128]{1,0:T(8,128)S(1)} %broadcast_add_fusion, pred[32,128]{1,0:T(8,128)(4,1)S(1)} %get-tuple-element.6), kind=kOutput, calls=%fused_computation.15 | convolution fusion | flops 1074266112 | bytes 25186304 | tf_op jit(solution)/shard_map/bsr,bsd->brd/dot_general | solution.py:148
  313.0 0.0 copy-start.1
  313.0 0.0 reduce-scatter.5.cloned.1.call-update
  313.0 185.0 %reduce-scatter.5.cloned.1.call-done = bf16[128,2048]{1,0:T(8,128)(2,1)} async-done(((bf16[4096,2048]{1,0:T(8,128)(2,1)}), bf16[128,2048]{1,0:T(8,128)(2,1)}) %reduce-scatter.5.cloned.1.call-update) | async-done | bytes 524304 | tf_op jit(solution)/shard_map/reduce_scatter | solution.py:109
  498.0 2.4 add_convert_fusion
  500.4 0.0 copy-done.1
  (7 shorter events, 0.1 us)
Async XLA Ops:
  6.5 272.2 %copy-start = (bf16[1,768,2048]{2,1,0:T(8,128)(2,1)S(1)}, bf16[1,768,2048]{2,1,0:T(8,128)(2,1)}, u32[]{:S(2)}) copy-start(bf16[1,768,2048]{2,1,0:T(8,128)(2,1)} %param.23) | copy-start | bytes 9437188
  6.5 40.7 %all-gather.3.cloned.1.call-start = ((), (), s32[]{:S(2)}) async-start(), calls=%async_computation.3 | async-start | bytes 2621440 | tf_op jit(solution)/shard_map/all_gather | solution.py:205
  8.6 131.0 %reduce-scatter.3.cloned.1.call-start = ((), (), s32[]{:S(2)}) async-start(), calls=%async_computation.4 | async-start | bytes 4718592 | tf_op jit(solution)/shard_map/reduce_scatter | solution.py:226
  49.0 1.6 copy-start.2
  50.6 1.2 copy-start.3
  51.8 89.3 %copy-start.4 = (f32[2048]{0:T(1024)S(1)}, f32[2048]{0:T(1024)}, u32[]{:S(2)}) copy-start(f32[2048]{0:T(1024)} %param.18) | copy-start | bytes 24580
  51.8 91.6 %copy-start.5 = (f32[128,8]{0,1:T(8,128)S(1)}, f32[128,8]{0,1:T(8,128)}, u32[]{:S(2)}) copy-start(f32[128,8]{0,1:T(8,128)} %param.20) | copy-start | bytes 12292
  51.8 91.6 %copy-start.6 = (s32[128,8]{0,1:T(8,128)S(1)}, s32[128,8]{0,1:T(8,128)}, u32[]{:S(2)}) copy-start(s32[128,8]{0,1:T(8,128)} %param.19) | copy-start | bytes 12292
  69.3 187.3 %all-gather.5.cloned.1.call-start = ((), (), s32[]{:S(2)}) async-start(), calls=%async_computation.5 | async-start | bytes 17301504 | tf_op jit(solution)/shard_map/all_gather | solution.py:105
  143.3 354.6 %reduce-scatter.5.cloned.1.call-start = ((), (), s32[]{:S(2)}) async-start(), calls=%async_computation.6 | async-start | bytes 17301504 | tf_op jit(solution)/shard_map/reduce_scatter | solution.py:109
  256.5 11.5 %copy-start.7 = (bf16[1,2048,768]{2,1,0:T(8,128)(2,1)S(1)}, bf16[1,2048,768]{2,1,0:T(8,128)(2,1)}, u32[]{:S(2)}) copy-start(bf16[1,2048,768]{2,1,0:T(8,128)(2,1)} %param.21) | copy-start | bytes 9437188
  313.0 187.4 %copy-start.1 = (bf16[1,768,2048]{2,1,0:T(8,128)(2,1)S(1)}, bf16[1,768,2048]{2,1,0:T(8,128)(2,1)}, u32[]{:S(2)}) copy-start(bf16[1,768,2048]{2,1,0:T(8,128)(2,1)} %param.23) | copy-start | bytes 9437188
Sparse Core Ops, SparseCore 0:
  9.2 38.0 all-gather.2
  69.4 70.1 reduce-scatter.2
  143.4 113.0 all-gather.4
  313.1 184.8 reduce-scatter.4

commit v2 on v1

--- a/solution.py
+++ b/solution.py
@@ -15,7 +15,10 @@
 QUERY_TILE = 256
 KEY_TILE = 256
 LOW = -1e30
-DENSE_BYTES = 32 * 1024 * 1024
+BITS = 5
+MESH = pl.DeviceIdType.MESH
+ORDERS = ((4, 1, 0, 3, 2), (4, 0, 3, 1, 2), (4, 3, 1, 0, 2), (4, 1, 3, 0, 2)) * 2
+EXP_ORDERS = ((4, 3, 2),) * 4
 
 
 def attention_kernel(
@@ -101,12 +104,172 @@
     )(bounds, queries, starts, keys, values, out_weight)
 
 
+def own_bits():
+    ctx = lax.axis_index("ctx")
+    exp = lax.axis_index("exp")
+    return (ctx // 2, ctx % 2, exp // 4, exp // 2 % 2, exp % 2)
+
+
+def partner(bits, bit):
+    b = [1 - value if at == bit else value for at, value in enumerate(bits)]
+    return (b[0] * 2 + b[1], b[2] * 4 + b[3] * 2 + b[4])
+
+
+def waves(chunks, stages):
+    for tick in range(stages + 2 * ((chunks - 1) // 4)):
+        for j in range(chunks):
+            stage = tick - j // 4 * 2
+            if 0 <= stage < stages:
+                yield j, stage
+
+
+def greet(bits, active):
+    barrier = pltpu.get_barrier_semaphore()
+    for bit in active:
+        pl.semaphore_signal(
+            barrier, inc=1, device_id=partner(bits, bit), device_id_type=MESH
+        )
+    pl.semaphore_wait(barrier, len(active))
+
+
+def gather_kernel(rows_ref, out_ref, local_sem, send_sem, recv_sem):
+    bits = own_bits()
+    chunks = len(ORDERS)
+    chunk = rows_ref.shape[1] // chunks
+    greet(bits, range(BITS))
+    local = pltpu.make_async_copy(rows_ref, out_ref.at[bits], local_sem)
+    local.start()
+    local.wait()
+    copies = {}
+
+    def begin(j, stage):
+        order = ORDERS[j][::-1]
+        held = order[:stage]
+        index = tuple(slice(None) if at in held else bits[at] for at in range(BITS))
+        part = out_ref.at[index + (slice(None), pl.ds(j * chunk, chunk))]
+        copies[j, stage] = pltpu.make_async_remote_copy(
+            src_ref=part,
+            dst_ref=part,
+            send_sem=send_sem.at[j, stage],
+            recv_sem=recv_sem.at[j, stage],
+            device_id=partner(bits, order[stage]),
+            device_id_type=MESH,
+        )
+        copies[j, stage].start()
+
+    for j in range(chunks):
+        begin(j, 0)
+    for j, stage in waves(chunks, BITS):
+        copies[j, stage].wait_recv()
+        if stage + 1 < BITS:
+            begin(j, stage + 1)
+    for copy in copies.values():
+        copy.wait_send()
+
+
 def gather_rows(rows):
-    return lax.all_gather(rows, ("ctx", "exp"), axis=0, tiled=True)
-
-
-def scatter_sum(partial):
-    return lax.psum_scatter(partial, ("ctx", "exp"), scatter_dimension=0, tiled=True)
+    return pl.pallas_call(
+        gather_kernel,
+        out_shape=jax.ShapeDtypeStruct((2,) * BITS + rows.shape, rows.dtype),
+        in_specs=[pl.BlockSpec(memory_space=pl.ANY)],
+        out_specs=pl.BlockSpec(memory_space=pl.ANY),
+        scratch_shapes=[
+            pltpu.SemaphoreType.DMA,
+            pltpu.SemaphoreType.DMA((len(ORDERS), BITS)),
+            pltpu.SemaphoreType.DMA((len(ORDERS), BITS)),
+        ],
+        compiler_params=pltpu.CompilerParams(collective_id=0, has_side_effects=True),
+    )(rows)
+
+
+def scatter_kernel(orders, partial_ref, out_ref, *scratch):
+    chunks = len(orders)
+    stages = len(orders[0])
+    active = sorted(orders[0])
+    landing = scratch[:stages]
+    send_sem, recv_sem = scratch[stages:]
+    bits = own_bits()
+    chunk = out_ref.shape[1] // chunks
+    greet(bits, active)
+    copies = {}
+
+    def held_ref(j, stage):
+        if stage == 0:
+            return lambda index: partial_ref.at[index + (slice(None), pl.ds(j * chunk, chunk))]
+        return lambda index: landing[stage - 1].at[(j,) + index]
+
+    def half(j, stage, value):
+        remaining = [at for at in active if at not in orders[j][:stage]]
+        bit = orders[j][stage]
+        return tuple(value if at == bit else slice(None) for at in remaining)
+
+    def begin(j, stage):
+        bit = orders[j][stage]
+        copies[j, stage] = pltpu.make_async_remote_copy(
+            src_ref=held_ref(j, stage)(half(j, stage, 1 - bits[bit])),
+            dst_ref=landing[stage].at[j],
+            send_sem=send_sem.at[j, stage],
+            recv_sem=recv_sem.at[j, stage],
+            device_id=partner(bits, bit),
+            device_id_type=MESH,
+        )
+        copies[j, stage].start()
+
+    def add(j, stage):
+        mine = held_ref(j, stage)
+        bit = orders[j][stage]
+        remaining = [at for at in active if at not in orders[j][:stage]]
+        arrived = landing[stage]
+        left = stages - 1 - stage
+
+        @pl.loop(0, 2**left)
+        def _(i):
+            place = tuple(i // 2 ** (left - 1 - k) % 2 for k in range(left))
+            spot = list(place)
+            spot.insert(remaining.index(bit), bits[bit])
+            total = arrived[(j,) + place].astype(jnp.float32) + mine(tuple(spot))[
+                ...
+            ].astype(jnp.float32)
+            if stage + 1 == stages:
+                out_ref[:, j * chunk : (j + 1) * chunk] = total.astype(out_ref.dtype)
+            else:
+                arrived[(j,) + place] = total.astype(arrived.dtype)
+
+    for j in range(chunks):
+        begin(j, 0)
+    for j, stage in waves(chunks, stages):
+        copies[j, stage].wait_recv()
+        add(j, stage)
+        if stage + 1 < stages:
+            begin(j, stage + 1)
+    for copy in copies.values():
+        copy.wait_send()
+
+
+def scatter_sum(partial, orders, collective_id):
+    rows, width = partial.shape
+    chunks = len(orders)
+    stages = len(orders[0])
+    own_rows = rows // 2**stages
+    return pl.pallas_call(
+        functools.partial(scatter_kernel, orders),
+        out_shape=jax.ShapeDtypeStruct((own_rows, width), partial.dtype),
+        in_specs=[pl.BlockSpec(memory_space=pltpu.VMEM)],
+        out_specs=pl.BlockSpec(memory_space=pltpu.VMEM),
+        scratch_shapes=[
+            pltpu.VMEM(
+                (chunks,) + (2,) * (stages - 1 - stage) + (own_rows, width // chunks), partial.dtype
+            )
+            for stage in range(stages)
+        ]
+        + [
+            pltpu.SemaphoreType.DMA((chunks, stages)),
+            pltpu.SemaphoreType.DMA((chunks, stages)),
+        ],
+        compiler_params=pltpu.CompilerParams(
+            collective_id=collective_id, has_side_effects=True, vmem_limit_bytes=52 * 1024 * 1024
+        ),
+    )(partial.reshape((2,) * stages + (own_rows, width)))
 
 
 def route_slots(expert_ids, route_weight, expert_count):
@@ -151,7 +314,7 @@
         weighted.reshape(expert_count, capacity, width),
         preferred_element_type=jnp.bfloat16,
     ).reshape(-1, width)
-    return scatter_sum(partial).astype(jnp.float32)
+    return scatter_sum(partial, ORDERS, 1).astype(jnp.float32)
 
 
 def slot_experts(
@@ -208,10 +371,13 @@
     all_segs = lax.all_gather(segment_ids, "ctx", axis=0, tiled=True)
 
     own_rows = residual.shape[0]
-    if expert_count * own_rows * residual.shape[1] * 2 <= DENSE_BYTES:
+    dense = (lax.axis_size("ctx"), lax.axis_size("exp")) == (4, 8)
+    if dense:
         pick, slot_weight = route_slots(expert_ids, route_weight, expert_count)
 
     starts = jnp.sum((all_segs[:, None] < segment_ids[None, :]).astype(jnp.int32), axis=0)
+    if dense:
+        starts, pick, slot_weight = lax.optimization_barrier((starts, pick, slot_weight))
     tile = min(QUERY_TILE, ctx_rows)
     begins = ctx_index * ctx_rows + jnp.arange(ctx_rows // tile, dtype=jnp.int32) * tile
     bounds = jnp.stack([starts[::tile] // KEY_TILE, (begins + tile - 1) // KEY_TILE + 1, begins])
@@ -223,15 +389,18 @@
         both[:, HEAD_DIM:],
         out_weight,
     )
-    attention_sum = lax.psum_scatter(
-        head_terms, "exp", scatter_dimension=0, tiled=True
-    ).astype(jnp.float32)
+    if dense:
+        attention_sum = scatter_sum(head_terms, EXP_ORDERS, 2).astype(jnp.float32)
+    else:
+        attention_sum = lax.psum_scatter(
+            head_terms, "exp", scatter_dimension=0, tiled=True
+        ).astype(jnp.float32)
     mixed_rows = residual.astype(jnp.float32) + attention_sum
     mean_square = jnp.mean(mixed_rows * mixed_rows, axis=-1, keepdims=True)
     normed = (mixed_rows * lax.rsqrt(mean_square + 1e-06) * norm_gain).astype(jnp.bfloat16)
     width = normed.shape[1]
 
-    if expert_count * own_rows * width * 2 <= DENSE_BYTES:
+    if dense:
         routed = dense_experts(normed, pick, slot_weight, gate_weight, up_weight, down_weight)
     else:
         routed = slot_experts(

time: 507 us -> 406 us (0.80)
  waiting for transfers between devices: 384 us -> 16.8 us
  Pallas kernels: 17.5 us -> 284 us
  blocking collectives: 19.4 us -> 8.68 us
  starting transfers between devices: 0.13 us -> 7.3 us
    pallas_call x0 -> x3, Pallas kernels: none -> 270 us  [the longest x1 136 us: gather_rows(): pl.pallas_call(gather_kernel, out_shape=jax.ShapeDtypeStruct((2,) * BITS...]
    reduce_scatter x2 -> x0, waiting for transfers between devices: 255 us -> none  [the longest x1 185 us: scatter_sum(): lax.psum_scatter(partial, ('ctx', 'exp'), scatter_dimension=0, tiled=True)]
    all_gather x1 -> x0, waiting for transfers between devices: 103 us -> none  [gather_rows(): return lax.all_gather(rows, ('ctx', 'exp'), axis=0, tiled=True)]
    all_to_all x1 -> x0, blocking collectives: 9.7 us -> none  [route_slots(): lax.all_to_all(route_table, ('ctx', 'exp'), split_axis=0, concat_axis=0,...]
    all_gather x1, waiting for transfers between devices: 26.1 us -> 16.7 us  [shards(): lax.all_gather(jnp.concatenate([my_keys, my_values], axis=1), 'ctx', axis...]
    all_to_all x0 -> x1, starting transfers between devices: none -> 7.3 us  [route_slots(): lax.all_to_all(route_table, ('ctx', 'exp'), split_axis=0, concat_axis=0,...]
  transfers between devices with their start and end apart: 4 -> 2, of which waited for: 4 -> 1; matrix products, arithmetic and copies ran while one was open for 1% -> 1% of each run, Pallas kernels for 0% -> 0%
where the time goes in v2:
time: 406 us; the launch traced here: 402 us
  Pallas kernels  284 us (70%)
  matrix products  57 us (14%)
  waiting for transfers between devices  16.8 us (4%)
  between operations  13.5 us (3%)
  other arithmetic  8.94 us (2%)
  blocking collectives  8.68 us (2%)
  starting transfers between devices  7.3 us (2%)
  local copies, waits for them, and re-layouts  6.44 us (2%)
    pallas_call x1, Pallas kernels, gather_rows(): pl.pallas_call(gather_kernel, out_shape=jax.ShapeDtypeStruct((2,) * BITS...  136 us
    pallas_call x2, Pallas kernels, scatter_sum(): pl.pallas_call(functools.partial(scatter_kernel, orders), out_shape=jax.S...  134 us
    dot_general x1, matrix products, apply_expert(): return jnp.dot(hidden, down_weight[0], preferred_element_type=jnp.float32)  20.8 us
    all_gather x1, waiting for transfers between devices, shards(): lax.all_gather(jnp.concatenate([my_keys, my_values], axis=1), 'ctx', axis...  16.7 us
    dot_general x1, matrix products, dense_experts(): jnp.einsum('bsr,bsd->brd', pick, weighted.reshape(expert_count, capacity,...  13.8 us
    pallas_call x1, Pallas kernels, attend(): pl.pallas_call(functools.partial(attention_kernel, tile, heads), out_shap...  13.7 us
    dot_general x1, matrix products, dense_experts(): jnp.einsum('bsr,brd->bsd', pick, everyone, preferred_element_type=jnp.bfl...  11.6 us
    dot_general x1, matrix products, apply_expert(): jnp.dot(arrived, gate_weight[0], preferred_element_type=jnp.float32)  10.7 us
  transfers between devices with their start and end apart: 2, of which 1 were waited for; matrix products, arithmetic and copies ran while one was open for 1% of the time, Pallas kernels for 0%

profile of v2, /device:TPU:0, one launch (start us, length us, event | category | flops | bytes accessed | tf_op | source)
XLA Modules:
  0.0 402.1 jit_solution(18218283513730358213)
XLA Ops:
  6.5 0.0 copy-start
  6.5 0.0 all-gather.2.cloned.1.call-start
  6.5 1.2 constant_dynamic-slice_fusion
  7.8 0.9 pad_maximum_fusion
  8.6 0.0 all-gather.2.cloned.1.call-update
  8.6 1.4 select_reduce_fusion.1
  10.0 7.3 %all-to-all-start = ((f32[32,1,128]{2,1,0:T(1,128)}), f32[32,1,128]{2,1,0:T(1,128)S(1)}, u32[]{:S(2)}, u32[]{:S(2)}) async-start(f32[32,1,128]{2,1,0:T(1,128)} %bitcast.1), calls=%async_computation | async-start | bytes 32768 | tf_op jit(solution)/shard_map/all_to_all | solution.py:281
  17.3 8.7 %all_gather.6 = s32[4096]{0:T(1024)S(1)} all-gather(s32[1024]{0:T(1024)} %param.16), channel_id=1, replica_groups=mesh['ctx'=4,'exp'=8] {'ctx'}, dimensions={0}, use_global_device_ids=true | all-gather | bytes 20480 | tf_op jit(solution)/shard_map/all_gather | solution.py:371
  26.0 2.6 convert_reduce_fusion
  28.6 0.0 all-to-all-done
  28.7 0.3 reduce_window_sum.14
  29.0 0.4 select_reduce_fusion
  29.4 1.0 fusion.7
  30.4 0.1 mul.71
  30.5 0.1 slice.9
  30.6 16.7 %all-gather.2.cloned.1.call-done = bf16[4096,256]{1,0:T(8,128)(2,1)} async-done(((bf16[1024,256]{1,0:T(8,128)(2,1)}), bf16[4096,256]{1,0:T(8,128)(2,1)}) %all-gather.2.cloned.1.call-update) | async-done | bytes 2097168 | tf_op jit(solution)/shard_map/all_gather | solution.py:368
  47.4 1.7 fusion.12
  49.0 0.0 copy-start.4
  49.0 1.6 copy-done.4
  50.6 0.0 copy-start.5
  50.6 1.2 copy-done.5
  51.9 0.0 copy-start.6
  51.9 0.0 copy-start.8
  51.9 13.7 %shard_map.118 = bf16[1024,2048]{1,0:T(8,128)(2,1)} custom-call(s32[3,4]{1,0:T(4,128)S(1)} %pad_add_fusion.bounds_ref, bf16[1024,512]{1,0:T(8,128)(2,1)S(1)} %copy-done.5, s32[1,1024]{1,0:T(1,128)S(1)} %bitcast.32, bf16[4096,128]{1,0:T(8,128)(2,1)S(1)} %get-tuple-element.14.k_ref, bf16[4096,128]{1,0:T(8,128)(2,1)S(1)} %get-tuple-element.13.v_ref, ...), custom_call_target="tpu_custom_call" | custom-call | tf_op jit(solution)/shard_map/pallas_call | solution.py:83
  65.5 45.8 %shard_map.119 = bf16[128,2048]{1,0:T(8,128)(2,1)S(1)} custom-call(bf16[2,2,2,128,2048]{4,3,2,1,0:T(8,128)(2,1)} %bitcast.38), custom_call_target="tpu_custom_call" | custom-call | tf_op jit(solution)/shard_map/pallas_call | solution.py:254
  111.3 0.0 copy-done.6
  111.3 0.0 copy-start.2
  111.3 0.3 multiply_reduce_fusion
  111.6 0.5 copy-done.2
  112.1 0.0 copy-done.8
  112.1 1.0 multiply_convert_fusion.2.rows_ref
  113.1 135.7 %shard_map.120 = bf16[2,2,2,2,2,128,2048]{6,5,4,3,2,1,0:T(8,128)(2,1)} custom-call(bf16[128,2048]{1,0:T(8,128)(2,1)} %multiply_convert_fusion.2.rows_ref), custom_call_target="tpu_custom_call" | custom-call | tf_op jit(solution)/shard_map/pallas_call | solution.py:171
  248.9 0.0 copy-start.9
  248.9 11.6 %fusion.13 = bf16[32,64,2048]{2,1,0:T(8,128)(2,1)} fusion(bf16[32,64,128]{2,1,0:T(8,128)(2,1)} %fusion.7, bf16[32,128,2048]{2,1,0:T(8,128)(2,1)} %bitcast.34), kind=kOutput, calls=%fused_computation.39 | convolution fusion | flops 1073741824 | bytes 25690112 | tf_op jit(solution)/shard_map/bsr,brd->bsd/dot_general | solution.py:306
  260.5 0.0 copy-done.9
  260.5 10.7 %fusion.3 = f32[2048,768]{1,0:T(8,128)} fusion(bf16[2048,2048]{1,0:T(8,128)(2,1)} %bitcast.36, bf16[1,2048,768]{2,1,0:T(8,128)(2,1)S(1)} %copy-done.9), kind=kOutput, calls=%fused_computation.5 | convolution fusion | flops 6442450944 | bytes 17825792 | tf_op jit(solution)/shard_map/dot_general | solution.py:296
  271.3 0.0 copy-done
  271.3 20.8 %multiply_convert_fusion = bf16[2048,2048]{1,0:T(8,128)(2,1)} fusion(f32[2048]{0:T(1024)S(1)} %mul.71, f32[2048,768]{1,0:T(8,128)} %fusion.3, bf16[2048,2048]{1,0:T(8,128)(2,1)} %bitcast.37, bf16[1,768,2048]{2,1,0:T(8,128)(2,1)S(1)} %copy-done, bf16[1,2048,768]{2,1,0:T(8,128)(2,1)} %param.22), kind=kOutput, calls=%fused_computation | convolution fusion | flops 12902727680 | bytes 29368320 | tf_op jit(solution)/shard_map/dot_general | solution.py:299
  292.0 13.8 %fusion.14 = bf16[32,128,2048]{2,1,0:T(8,128)(2,1)} fusion(bf16[32,64,128]{2,1,0:T(8,128)(2,1)} %fusion.7, bf16[32,64,2048]{2,1,0:T(8,128)(2,1)} %bitcast.35), kind=kOutput, calls=%fused_computation.40 | convolution fusion | flops 1073741824 | bytes 25690112 | tf_op jit(solution)/shard_map/bsr,bsd->brd/dot_general | solution.py:311
  305.8 0.0 copy-start.1
  305.8 0.0 copy-start.3
  305.9 0.0 copy-start.7
  305.9 88.4 %shard_map.121 = bf16[128,2048]{1,0:T(8,128)(2,1)S(1)} custom-call(bf16[2,2,2,2,2,128,2048]{6,5,4,3,2,1,0:T(8,128)(2,1)} %bitcast.33), custom_call_target="tpu_custom_call" | custom-call | tf_op jit(solution)/shard_map/pallas_call | solution.py:254
  394.2 0.0 copy-done.3
  394.2 0.0 copy-done.7
  394.3 1.0 add_convert_fusion
  395.3 0.0 copy-done.1
  (6 shorter events, 0.1 us)
Async XLA Ops:
  6.5 264.7 %copy-start = (bf16[1,768,2048]{2,1,0:T(8,128)(2,1)S(1)}, bf16[1,768,2048]{2,1,0:T(8,128)(2,1)}, u32[]{:S(2)}) copy-start(bf16[1,768,2048]{2,1,0:T(8,128)(2,1)} %param.23) | copy-start | bytes 9437188
  6.5 40.8 %all-gather.2.cloned.1.call-start = ((), (), s32[]{:S(2)}) async-start(), calls=%async_computation.1 | async-start | bytes 2621440 | tf_op jit(solution)/shard_map/all_gather | solution.py:368
  10.0 18.7 %all-to-all-start = ((f32[32,1,128]{2,1,0:T(1,128)}), f32[32,1,128]{2,1,0:T(1,128)S(1)}, u32[]{:S(2)}, u32[]{:S(2)}) async-start(f32[32,1,128]{2,1,0:T(1,128)} %bitcast.1), calls=%async_computation | async-start | bytes 32768 | tf_op jit(solution)/shard_map/all_to_all | solution.py:281
  49.0 1.6 copy-start.4
  50.6 1.2 copy-start.5
  51.9 59.4 %copy-start.6 = (bf16[128,2048]{1,0:T(8,128)(2,1)S(1)}, bf16[128,2048]{1,0:T(8,128)(2,1)}, u32[]{:S(2)}) copy-start(bf16[128,2048]{1,0:T(8,128)(2,1)} %param.12) | copy-start | bytes 1572868
  51.9 60.3 %copy-start.8 = (f32[2048]{0:T(1024)S(1)}, f32[2048]{0:T(1024)}, u32[]{:S(2)}) copy-start(f32[2048]{0:T(1024)} %param.18) | copy-start | bytes 24580
  111.3 0.8 copy-start.2
  248.9 11.7 %copy-start.9 = (bf16[1,2048,768]{2,1,0:T(8,128)(2,1)S(1)}, bf16[1,2048,768]{2,1,0:T(8,128)(2,1)}, u32[]{:S(2)}) copy-start(bf16[1,2048,768]{2,1,0:T(8,128)(2,1)} %param.21) | copy-start | bytes 9437188
  305.8 89.4 %copy-start.1 = (bf16[1,768,2048]{2,1,0:T(8,128)(2,1)S(1)}, bf16[1,768,2048]{2,1,0:T(8,128)(2,1)}, u32[]{:S(2)}) copy-start(bf16[1,768,2048]{2,1,0:T(8,128)(2,1)} %param.23) | copy-start | bytes 9437188
  305.8 88.4 %copy-start.3 = (bf16[128,2048]{1,0:T(8,128)(2,1)S(1)}, bf16[128,2048]{1,0:T(8,128)(2,1)}, u32[]{:S(2)}) copy-start(bf16[128,2048]{1,0:T(8,128)(2,1)} %copy-done.2) | copy-start | bytes 1572868
  305.9 88.4 %copy-start.7 = (bf16[128,2048]{1,0:T(8,128)(2,1)S(1)}, bf16[128,2048]{1,0:T(8,128)(2,1)}, u32[]{:S(2)}) copy-start(bf16[128,2048]{1,0:T(8,128)(2,1)} %param.12) | copy-start | bytes 1572868
Sparse Core Ops, SparseCore 0:
  9.2 38.1 all-gather.1

commit v3 on v2

--- a/solution.py
+++ b/solution.py
@@ -42,28 +42,42 @@
         values = v_ref[pl.ds(key_begin, KEY_TILE), :]
         key_pos = key_begin + lax.broadcasted_iota(jnp.int32, (KEY_TILE, 1), 0)
         visible = (key_pos >= starts) & (key_pos <= query_pos)
-        for head in range(heads):
-            query = q_ref[:, head * HEAD_DIM : (head + 1) * HEAD_DIM]
-            scores = lax.dot_general(
-                keys, query, (((1,), (1,)), ((), ())), preferred_element_type=jnp.float32
+        scores = [
+            lax.dot_general(
+                keys,
+                q_ref[:, head * HEAD_DIM : (head + 1) * HEAD_DIM],
+                (((1,), (1,)), ((), ())),
+                preferred_element_type=jnp.float32,
             )
-            scores = jnp.where(visible, scores * scale, LOW * 2)
-            old_max = m_ref[head : head + 1, :]
-            new_max = jnp.maximum(old_max, jnp.max(scores, axis=0, keepdims=True))
-            rescale = jnp.exp2(old_max - new_max)
-            unnormed = jnp.exp2(scores - new_max)
-            l_ref[head : head + 1, :] = l_ref[head : head + 1, :] * rescale + jnp.sum(
-                unnormed, axis=0, keepdims=True
-            )
-            m_ref[head : head + 1, :] = new_max
-            gained = lax.dot_general(
+            for head in range(heads)
+        ]
+        scores = [jnp.where(visible, part * scale, LOW * 2) for part in scores]
+        old_max = m_ref[...]
+        old_total = l_ref[...]
+        new_max = jnp.maximum(
+            old_max,
+            jnp.concatenate([jnp.max(part, axis=0, keepdims=True) for part in scores], axis=0),
+        )
+        rescale = jnp.exp2(old_max - new_max)
+        unnormed = [
+            jnp.exp2(part - new_max[head : head + 1, :]) for head, part in enumerate(scores)
+        ]
+        gained = [
+            lax.dot_general(
                 values,
-                unnormed.astype(jnp.bfloat16),
+                part.astype(jnp.bfloat16),
                 (((0,), (0,)), ((), ())),
                 preferred_element_type=jnp.float32,
             )
+            for part in unnormed
+        ]
+        m_ref[...] = new_max
+        l_ref[...] = old_total * rescale + jnp.concatenate(
+            [jnp.sum(part, axis=0, keepdims=True) for part in unnormed], axis=0
+        )
+        for head in range(heads):
             rows = slice(head * HEAD_DIM, (head + 1) * HEAD_DIM)
-            acc_ref[rows, :] = acc_ref[rows, :] * rescale + gained
+            acc_ref[rows, :] = acc_ref[rows, :] * rescale[head : head + 1, :] + gained[head]
 
     for head in range(heads):
         rows = slice(head * HEAD_DIM, (head + 1) * HEAD_DIM)
@@ -171,14 +185,16 @@
     return pl.pallas_call(
         gather_kernel,
         out_shape=jax.ShapeDtypeStruct((2,) * BITS + rows.shape, rows.dtype),
-        in_specs=[pl.BlockSpec(memory_space=pl.ANY)],
-        out_specs=pl.BlockSpec(memory_space=pl.ANY),
+        in_specs=[pl.BlockSpec(memory_space=pltpu.VMEM)],
+        out_specs=pl.BlockSpec(memory_space=pltpu.VMEM),
         scratch_shapes=[
             pltpu.SemaphoreType.DMA,
             pltpu.SemaphoreType.DMA((len(ORDERS), BITS)),
             pltpu.SemaphoreType.DMA((len(ORDERS), BITS)),
         ],
-        compiler_params=pltpu.CompilerParams(collective_id=0, has_side_effects=True),
+        compiler_params=pltpu.CompilerParams(
+            collective_id=0, has_side_effects=True, vmem_limit_bytes=40 * 1024 * 1024
+        ),
     )(rows)
 
 

time: 406 us -> 376 us (0.926)
  Pallas kernels: 284 us -> 257 us
    pallas_call x1, Pallas kernels: 136 us -> 112 us  [gather_rows(): pl.pallas_call(gather_kernel, out_shape=jax.ShapeDtypeStruct((2,) * BITS...]
  transfers between devices with their start and end apart: 2 -> 2, of which waited for: 1 -> 1; matrix products, arithmetic and copies ran while one was open for 1% -> 2% of each run, Pallas kernels for 0% -> 0%
where the time goes in v3:
time: 376 us; the launch traced here: 374 us
  Pallas kernels  257 us (68%)
  matrix products  56.9 us (15%)
  waiting for transfers between devices  16.8 us (4%)
  between operations  13.6 us (4%)
  blocking collectives  8.68 us (2%)
  other arithmetic  8.15 us (2%)
  starting transfers between devices  7.3 us (2%)
  local copies, waits for them, and re-layouts  5.91 us (2%)
    pallas_call x2, Pallas kernels, scatter_sum(): pl.pallas_call(functools.partial(scatter_kernel, orders), out_shape=jax.S...  134 us
    pallas_call x1, Pallas kernels, gather_rows(): pl.pallas_call(gather_kernel, out_shape=jax.ShapeDtypeStruct((2,) * BITS...  112 us
    dot_general x1, matrix products, apply_expert(): return jnp.dot(hidden, down_weight[0], preferred_element_type=jnp.float32)  20.8 us
    all_gather x1, waiting for transfers between devices, shards(): lax.all_gather(jnp.concatenate([my_keys, my_values], axis=1), 'ctx', axis...  16.7 us
    dot_general x1, matrix products, dense_experts(): jnp.einsum('bsr,bsd->brd', pick, weighted.reshape(expert_count, capacity,...  13.8 us
    dot_general x1, matrix products, dense_experts(): jnp.einsum('bsr,brd->bsd', pick, everyone, preferred_element_type=jnp.bfl...  11.5 us
    dot_general x1, matrix products, apply_expert(): jnp.dot(arrived, gate_weight[0], preferred_element_type=jnp.float32)  10.7 us
    pallas_call x1, Pallas kernels, attend(): pl.pallas_call(functools.partial(attention_kernel, tile, heads), out_shap...  10.6 us
  transfers between devices with their start and end apart: 2, of which 1 were waited for; matrix products, arithmetic and copies ran while one was open for 2% of the time, Pallas kernels for 0%

profile of v3, /device:TPU:0, one launch (start us, length us, event | category | flops | bytes accessed | tf_op | source)
XLA Modules:
  0.0 373.8 jit_solution(5570806525142678646)
XLA Ops:
  6.5 0.0 copy-start
  6.5 0.0 all-gather.2.cloned.1.call-start
  6.5 1.2 constant_dynamic-slice_fusion
  7.8 0.8 pad_maximum_fusion
  8.6 0.0 all-gather.2.cloned.1.call-update
  8.6 1.4 select_reduce_fusion.1
  10.0 7.3 %all-to-all-start = ((f32[32,1,128]{2,1,0:T(1,128)}), f32[32,1,128]{2,1,0:T(1,128)S(1)}, u32[]{:S(2)}, u32[]{:S(2)}) async-start(f32[32,1,128]{2,1,0:T(1,128)} %bitcast.1), calls=%async_computation | async-start | bytes 32768 | tf_op jit(solution)/shard_map/all_to_all | solution.py:297
  17.3 8.7 %all_gather.6 = s32[4096]{0:T(1024)S(1)} all-gather(s32[1024]{0:T(1024)} %param.16), channel_id=1, replica_groups=mesh['ctx'=4,'exp'=8] {'ctx'}, dimensions={0}, use_global_device_ids=true | all-gather | bytes 20480 | tf_op jit(solution)/shard_map/all_gather | solution.py:387
  26.0 2.6 convert_reduce_fusion
  28.6 0.0 all-to-all-done
  28.7 0.3 reduce_window_sum.14
  29.0 0.4 select_reduce_fusion
  29.4 1.0 fusion.7
  30.4 0.1 mul.71
  30.5 0.1 slice.9
  30.6 16.7 %all-gather.2.cloned.1.call-done = bf16[4096,256]{1,0:T(8,128)(2,1)} async-done(((bf16[1024,256]{1,0:T(8,128)(2,1)}), bf16[4096,256]{1,0:T(8,128)(2,1)}) %all-gather.2.cloned.1.call-update) | async-done | bytes 2097168 | tf_op jit(solution)/shard_map/all_gather | solution.py:384
  47.4 1.7 fusion.12
  49.0 0.0 copy-start.4
  49.0 1.6 copy-done.4
  50.6 0.0 copy-start.5
  50.6 1.2 copy-done.5
  51.9 0.0 copy-start.7
  51.9 0.0 copy-start.9
  51.9 10.6 %shard_map.118 = bf16[1024,2048]{1,0:T(8,128)(2,1)} custom-call(s32[3,4]{1,0:T(4,128)S(1)} %pad_add_fusion.bounds_ref, bf16[1024,512]{1,0:T(8,128)(2,1)S(1)} %copy-done.5, s32[1,1024]{1,0:T(1,128)S(1)} %bitcast.32, bf16[4096,128]{1,0:T(8,128)(2,1)S(1)} %get-tuple-element.14.k_ref, bf16[4096,128]{1,0:T(8,128)(2,1)S(1)} %get-tuple-element.13.v_ref, ...), custom_call_target="tpu_custom_call" | custom-call | tf_op jit(solution)/shard_map/pallas_call | solution.py:97
  62.5 45.8 %shard_map.119 = bf16[128,2048]{1,0:T(8,128)(2,1)S(1)} custom-call(bf16[2,2,2,128,2048]{4,3,2,1,0:T(8,128)(2,1)} %bitcast.38), custom_call_target="tpu_custom_call" | custom-call | tf_op jit(solution)/shard_map/pallas_call | solution.py:270
  108.2 0.0 copy-done.7
  108.3 0.0 copy-start.2
  108.3 0.3 multiply_reduce_fusion
  108.5 0.0 copy-done.9
  108.5 0.2 multiply_convert_fusion.2.rows_ref
  108.8 0.0 copy-start.6
  108.8 111.8 %shard_map.120 = bf16[2,2,2,2,2,128,2048]{6,5,4,3,2,1,0:T(8,128)(2,1)} custom-call(bf16[128,2048]{1,0:T(8,128)(2,1)S(1)} %multiply_convert_fusion.2.rows_ref), custom_call_target="tpu_custom_call" | custom-call | tf_op jit(solution)/shard_map/pallas_call | solution.py:185
  220.6 0.0 copy-done.2
  220.6 0.0 copy-done.6
  220.6 0.0 copy-start.10
  220.6 11.5 %fusion.13 = bf16[32,64,2048]{2,1,0:T(8,128)(2,1)} fusion(bf16[32,64,128]{2,1,0:T(8,128)(2,1)S(1)} %copy-done.6, bf16[32,128,2048]{2,1,0:T(8,128)(2,1)} %bitcast.34), kind=kOutput, calls=%fused_computation.39 | convolution fusion | flops 1073741824 | bytes 25690112 | tf_op jit(solution)/shard_map/bsr,brd->bsd/dot_general | solution.py:322
  232.2 0.0 copy-done.10
  232.2 10.7 %fusion.3 = f32[2048,768]{1,0:T(8,128)} fusion(bf16[2048,2048]{1,0:T(8,128)(2,1)} %bitcast.36, bf16[1,2048,768]{2,1,0:T(8,128)(2,1)S(1)} %copy-done.10), kind=kOutput, calls=%fused_computation.5 | convolution fusion | flops 6442450944 | bytes 17825792 | tf_op jit(solution)/shard_map/dot_general | solution.py:312
  242.9 0.0 copy-done
  242.9 20.8 %multiply_convert_fusion = bf16[2048,2048]{1,0:T(8,128)(2,1)} fusion(f32[2048]{0:T(1024)S(1)} %mul.71, f32[2048,768]{1,0:T(8,128)} %fusion.3, bf16[2048,2048]{1,0:T(8,128)(2,1)} %bitcast.37, bf16[1,768,2048]{2,1,0:T(8,128)(2,1)S(1)} %copy-done, bf16[1,2048,768]{2,1,0:T(8,128)(2,1)} %param.22), kind=kOutput, calls=%fused_computation | convolution fusion | flops 12902727680 | bytes 29368320 | tf_op jit(solution)/shard_map/dot_general | solution.py:315
  263.6 13.8 %fusion.14 = bf16[32,128,2048]{2,1,0:T(8,128)(2,1)} fusion(bf16[32,64,128]{2,1,0:T(8,128)(2,1)} %fusion.7, bf16[32,64,2048]{2,1,0:T(8,128)(2,1)} %bitcast.35), kind=kOutput, calls=%fused_computation.40 | convolution fusion | flops 1073741824 | bytes 25690112 | tf_op jit(solution)/shard_map/bsr,bsd->brd/dot_general | solution.py:327
  277.5 0.0 copy-start.1
  277.5 0.0 copy-start.3
  277.5 0.0 copy-start.8
  277.5 88.4 %shard_map.121 = bf16[128,2048]{1,0:T(8,128)(2,1)S(1)} custom-call(bf16[2,2,2,2,2,128,2048]{6,5,4,3,2,1,0:T(8,128)(2,1)} %bitcast.33), custom_call_target="tpu_custom_call" | custom-call | tf_op jit(solution)/shard_map/pallas_call | solution.py:270
  365.9 0.0 copy-done.3
  365.9 0.0 copy-done.8
  365.9 1.0 add_convert_fusion
  366.9 0.0 copy-done.1
  (6 shorter events, 0.1 us)
Async XLA Ops:
  6.5 236.3 %copy-start = (bf16[1,768,2048]{2,1,0:T(8,128)(2,1)S(1)}, bf16[1,768,2048]{2,1,0:T(8,128)(2,1)}, u32[]{:S(2)}) copy-start(bf16[1,768,2048]{2,1,0:T(8,128)(2,1)} %param.23) | copy-start | bytes 9437188
  6.5 40.8 %all-gather.2.cloned.1.call-start = ((), (), s32[]{:S(2)}) async-start(), calls=%async_computation.1 | async-start | bytes 2621440 | tf_op jit(solution)/shard_map/all_gather | solution.py:384
  10.0 18.7 %all-to-all-start = ((f32[32,1,128]{2,1,0:T(1,128)}), f32[32,1,128]{2,1,0:T(1,128)S(1)}, u32[]{:S(2)}, u32[]{:S(2)}) async-start(f32[32,1,128]{2,1,0:T(1,128)} %bitcast.1), calls=%async_computation | async-start | bytes 32768 | tf_op jit(solution)/shard_map/all_to_all | solution.py:297
  49.0 1.6 copy-start.4
  50.6 1.2 copy-start.5
  51.9 56.4 %copy-start.7 = (bf16[128,2048]{1,0:T(8,128)(2,1)S(1)}, bf16[128,2048]{1,0:T(8,128)(2,1)}, u32[]{:S(2)}) copy-start(bf16[128,2048]{1,0:T(8,128)(2,1)} %param.12) | copy-start | bytes 1572868
  51.9 56.7 %copy-start.9 = (f32[2048]{0:T(1024)S(1)}, f32[2048]{0:T(1024)}, u32[]{:S(2)}) copy-start(f32[2048]{0:T(1024)} %param.18) | copy-start | bytes 24580
  108.3 112.3 %copy-start.2 = (bf16[128,2048]{1,0:T(8,128)(2,1)}, bf16[128,2048]{1,0:T(8,128)(2,1)S(1)}, u32[]{:S(2)}) copy-start(bf16[128,2048]{1,0:T(8,128)(2,1)S(1)} %shard_map.119) | copy-start | bytes 1572868
  108.8 111.8 %copy-start.6 = (bf16[32,64,128]{2,1,0:T(8,128)(2,1)S(1)}, bf16[32,64,128]{2,1,0:T(8,128)(2,1)}, u32[]{:S(2)}) copy-start(bf16[32,64,128]{2,1,0:T(8,128)(2,1)} %fusion.7) | copy-start | bytes 1572868
  220.6 11.6 %copy-start.10 = (bf16[1,2048,768]{2,1,0:T(8,128)(2,1)S(1)}, bf16[1,2048,768]{2,1,0:T(8,128)(2,1)}, u32[]{:S(2)}) copy-start(bf16[1,2048,768]{2,1,0:T(8,128)(2,1)} %param.21) | copy-start | bytes 9437188
  277.5 89.5 %copy-start.1 = (bf16[1,768,2048]{2,1,0:T(8,128)(2,1)S(1)}, bf16[1,768,2048]{2,1,0:T(8,128)(2,1)}, u32[]{:S(2)}) copy-start(bf16[1,768,2048]{2,1,0:T(8,128)(2,1)} %param.23) | copy-start | bytes 9437188
  277.5 88.4 %copy-start.3 = (bf16[128,2048]{1,0:T(8,128)(2,1)S(1)}, bf16[128,2048]{1,0:T(8,128)(2,1)}, u32[]{:S(2)}) copy-start(bf16[128,2048]{1,0:T(8,128)(2,1)} %copy-done.2) | copy-start | bytes 1572868
  277.5 88.4 %copy-start.8 = (bf16[128,2048]{1,0:T(8,128)(2,1)S(1)}, bf16[128,2048]{1,0:T(8,128)(2,1)}, u32[]{:S(2)}) copy-start(bf16[128,2048]{1,0:T(8,128)(2,1)} %param.12) | copy-start | bytes 1572868
Sparse Core Ops, SparseCore 0:
  9.2 38.1 all-gather.1
